TPU v7x, 32 devices: a whole 2x2x4 slice. The times are simulated.
32 devices in a mesh: parts: 2 (over x), dp: 2 (over core), tensor: 8 (over z, y).
Axes of the slice: x: 2, y: 2, z: 4, core: 2. Of those that a mesh axis runs over, the one named last changes fastest.
Arguments:
- query: bfloat16 [512, 8192], P(('parts', 'dp'), 'tensor'), parts along dimension 0, may hold values from -80 to 80
- step_key_value: bfloat16 [512, 8, 256], P(('parts', 'dp'), 'tensor'), parts along dimension 0, may hold values from -4 to 4, as said below
- cache: bfloat16 [512, 128, 8, 256], P(('parts', 'dp'), None, 'tensor'), parts along dimension 0, may hold values from -4 to 4, as said below
- output_projection_weight: bfloat16 [8192, 8192], P('tensor'), may hold values from -0.0625 to 0.0625
- adapter_down_weight: bfloat16 [8192, 128, 64], P('tensor', 'dp'), may hold values from -0.0625 to 0.0625
- adapter_up_weight: bfloat16 [128, 64, 8192], P('dp', None, 'tensor'), may hold values from -0.75 to 0.75
- row_adapter_index: int32 [512], P('parts'), parts along dimension 0, may hold values from 0 to 127
- adapter_storage_slot: int32 [128], replicated, may hold values from 0 to 127, each once
Outputs:
- mixed: bfloat16 [512, 8192], P(('parts', 'dp'), 'tensor'), parts along dimension 0
There are 2 independent parts, one for each index of `parts`. A program takes and returns all parts, laid end to end along the dimension named above; an argument that names none is the same for every part. Nothing has to cross between parts.
Inputs may be any that keep to these rules, and one draw needn't show every extreme that they name: `cache`: copies c and c' are equal where c * 1 = c' * 8 // 8. `step_key_value`: copies c and c' are equal where c * 1 = c' * 8 // 8. `adapter_storage_slot`: each slot holds exactly one adapter.
All inputs are finite; a program needn't handle non-finite values.
Results may differ from a plain program's by a relative error of at most 0.0061.
Values may be sent and summed in bfloat16 or wider, within the bound.
A program may use at most 128 MiB of HBM per device.

v0:
```python
import math

import jax
import jax.numpy as jnp
from jax import lax
from jax.sharding import PartitionSpec as P


def attend(query, step_key_value, cache):
    row_count = query.shape[0]
    copies = cache.shape[2]
    head_width = cache.shape[3] // 2
    group = query.shape[1] // (copies * head_width)
    heads = query.reshape(row_count, copies, group, head_width)
    score_scale = 1.0 / math.sqrt(head_width)
    scores = (
        jnp.einsum(
            "rsgd,rcsd->rsgc", heads, cache[..., :head_width], preferred_element_type=jnp.float32
        )
        * score_scale
    )
    own_score = (
        jnp.einsum(
            "rsgd,rsd->rsg",
            heads,
            step_key_value[..., :head_width],
            preferred_element_type=jnp.float32,
        )
        * score_scale
    )
    peak = jnp.maximum(jnp.max(scores, axis=-1), own_score)
    expos = jnp.exp(scores - peak[..., None])
    own_expo = jnp.exp(own_score - peak)
    total = jnp.sum(expos, axis=-1) + own_expo
    weights = (expos / total[..., None]).astype(jnp.bfloat16)
    own_weight = (own_expo / total).astype(jnp.bfloat16)
    summed = jnp.einsum(
        "rsgc,rcsd->rsgd", weights, cache[..., head_width:], preferred_element_type=jnp.float32
    )
    summed = summed + own_weight.astype(jnp.float32)[..., None] * step_key_value[
        :, :, None, head_width:
    ].astype(jnp.float32)
    return summed.astype(jnp.bfloat16).reshape(row_count, -1)


def rank_delta(features, local_slot, down_flat, up_flat, slot_count):
    row_count = features.shape[0]
    rank_width = down_flat.shape[1] // slot_count
    partial_value = jnp.dot(features, down_flat, preferred_element_type=jnp.float32).reshape(
        row_count, slot_count, rank_width
    )
    one_hot = local_slot[:, None] == jnp.arange(slot_count, dtype=jnp.int32)[None, :]
    picked = jnp.sum(jnp.where(one_hot[:, :, None], partial_value, 0.0), axis=1)
    low = lax.psum(picked, "tensor").astype(jnp.bfloat16)
    widened_rows = jnp.where(one_hot[:, :, None], low[:, None, :], jnp.zeros((), jnp.bfloat16))
    widened_rows = widened_rows.reshape(row_count, slot_count * rank_width)
    return jnp.dot(widened_rows, up_flat, preferred_element_type=jnp.float32)


def on_device(
    query,
    step_key_value,
    cache,
    output_projection_weight,
    adapter_down_weight,
    adapter_up_weight,
    row_adapter_index,
    adapter_storage_slot,
):
    attention_result = attend(query, step_key_value, cache)
    row_count = attention_result.shape[0]
    feature_cols = attention_result.shape[1]
    base = lax.psum_scatter(
        lax.dot_general(
            output_projection_weight,
            attention_result,
            (((0,), (1,)), ((), ())),
            preferred_element_type=jnp.float32,
        ),
        "tensor",
        scatter_dimension=0,
        tiled=True,
    ).T
    adapter_total = adapter_storage_slot.shape[0]
    matches = row_adapter_index[:, None] == jnp.arange(adapter_total, dtype=jnp.int32)[None, :]
    slot_all = jnp.sum(jnp.where(matches, adapter_storage_slot[None, :], 0), axis=1)
    replicas = lax.axis_size("dp")
    my_replica = lax.axis_index("dp")
    slots_here = adapter_up_weight.shape[0]
    my_slots = lax.dynamic_slice_in_dim(slot_all, my_replica * row_count, row_count)
    owner = my_slots // slots_here
    targets = jnp.arange(replicas, dtype=jnp.int32)
    outgoing = jnp.where(
        owner[None, :, None] == targets[:, None, None],
        attention_result[None],
        jnp.zeros((), jnp.bfloat16),
    )
    incoming = lax.all_to_all(outgoing, "dp", split_axis=0, concat_axis=0, tiled=True)
    local_slot = slot_all % slots_here
    down_flat = adapter_down_weight.reshape(adapter_down_weight.shape[0], -1)
    up_flat = adapter_up_weight.reshape(-1, adapter_up_weight.shape[2])
    terms = rank_delta(
        incoming.reshape(replicas * row_count, feature_cols),
        local_slot,
        down_flat,
        up_flat,
        slots_here,
    )
    terms = terms.reshape(replicas, row_count, -1)
    returned = lax.all_to_all(terms, "dp", split_axis=0, concat_axis=0, tiled=True)
    adapter_update = jnp.sum(returned, axis=0)
    return (base + adapter_update).astype(jnp.bfloat16)


def solution(mesh):
    in_specs = (
        P(("parts", "dp"), "tensor"),
        P(("parts", "dp"), "tensor", None),
        P(("parts", "dp"), None, "tensor", None),
        P("tensor", None),
        P("tensor", "dp", None),
        P("dp", None, "tensor"),
        P("parts"),
        P(),
    )
    out_specs = P(("parts", "dp"), "tensor")
    return jax.shard_map(
        on_device, mesh=mesh, in_specs=in_specs, out_specs=out_specs, check_vma=False
    )
```

profile of v0, /device:TPU:0, one launch (start us, length us, event | category | flops | bytes accessed | tf_op | source)
XLA Modules:
  0.0 129.2 jit_solution(4208440946584927107)
XLA Ops:
  6.5 0.8 slice_bitcast_fusion.10
  7.3 1.0 copy.31
  8.3 0.3 fusion.15
  8.6 4.5 %fusion.21 = (f32[128,8]{1,0:T(8,128)S(1)}, f32[128,8,128]{2,1,0:T(8,128)S(1)}) fusion(bf16[128,8,128]{2,1,0:T(8,128)(2,1)S(1)} %bitcast.77, bf16[128,128,1,256]{3,1,0,2:T(8,128)(2,1)} %bitcast.74), kind=kOutput, calls=%fused_computation.45 | convolution fusion | flops 33815552 | bytes 4984832 | tf_op jit(solution)/shard_map/rsgd,rcsd->rsgc/dot_general | solution.py:17
  13.3 0.1 copy.23
  13.4 0.4 fusion.12
  13.8 0.1 copy.25
  14.0 0.1 copy.27
  14.1 3.4 %fusion.10 = bf16[128,8,128]{2,1,0:T(8,128)(2,1)S(1)} fusion(bf16[128,128,1,256]{3,1,0,2:T(8,128)(2,1)} %bitcast.75, f32[128,8,128]{2,1,0:T(8,128)S(1)} %get-tuple-element.10, f32[128,128]{1,0:T(8,128)S(1)} %get-tuple-element.6, f32[128,8]{1,0:T(8,128)S(1)} %copy.27, f32[128,8]{1,0:T(8,128)S(1)} %copy.25, f32[128,8]{1,0:T(8,128)S(1)} %copy.23), kind=kOutput, calls=%fused_computation.13 | convolution fusion | flops 34340864 | bytes 5058560 | tf_op jit(solution)/shard_map/rsgc,rcsd->rsgd/dot_general | solution.py:37
  17.5 10.1 %convolution_bitcast_fusion = f32[8192,128]{0,1:T(8,128)} fusion(bf16[1024,8192]{1,0:T(8,128)(2,1)} %param.11, bf16[16,8,8,128]{3,2,1,0:T(8,128)(2,1)S(1)} %bitcast.79), kind=kOutput, calls=%fused_computation | convolution fusion | flops 2147483648 | bytes 21233664 | tf_op jit(solution)/shard_map/dot_general | solution.py:74
  27.7 0.6 copy-done
  28.3 0.2 select_reduce_fusion.1
  28.5 0.9 broadcast_select_fusion.1
  29.4 3.5 %all-to-all-start = ((bf16[2,128,1024]{2,1,0:T(8,128)(2,1)}), bf16[2,128,1024]{2,1,0:T(8,128)(2,1)S(1)}, u32[]{:S(2)}, u32[]{:S(2)}) async-start(bf16[2,128,1024]{2,1,0:T(8,128)(2,1)} %broadcast_select_fusion.1), calls=%async_computation.1 | async-start | bytes 1048576 | tf_op jit(solution)/shard_map/all_to_all | solution.py:98
  33.0 1.7 %all-to-all-done = bf16[2,128,1024]{2,1,0:T(8,128)(2,1)S(1)} async-done(((bf16[2,128,1024]{2,1,0:T(8,128)(2,1)}), bf16[2,128,1024]{2,1,0:T(8,128)(2,1)S(1)}, u32[]{:S(2)}, u32[]{:S(2)}) %all-to-all-start) | async-done | bytes 524320 | tf_op jit(solution)/shard_map/all_to_all | solution.py:98
  34.7 6.1 %select_reduce_fusion = f32[256,64]{0,1:T(8,128)S(1)} fusion(pred[256,64]{0,1:T(8,128)(4,1)S(1)} %iota_compare_fusion.1, bf16[256,1024,1]{1,0,2:T(8,128)(2,1)S(1)} %bitcast.81, bf16[1024,64,64]{0,2,1:T(8,128)(2,1)} %param.12), kind=kOutput, calls=%fused_computation.7 | convolution fusion | flops 2149564416 | bytes 8994816 | tf_op jit(solution)/shard_map/dot_general | solution.py:49
  40.8 41.1 %psum.7 = bf16[256,64]{0,1:T(8,128)(2,1)S(1)} all-reduce(f32[256,64]{0,1:T(8,128)S(1)} %select_reduce_fusion), channel_id=1, replica_groups=mesh['parts'=2,'dp'=2,'tensor'=8] {'tensor'}, use_global_device_ids=true, to_apply=%region_5.6 | all-reduce | flops 16384 | bytes 98304 | tf_op jit(solution)/shard_map/psum | solution.py:54
  81.9 1.5 %broadcast_select_fusion = bf16[256,64,64]{0,2,1:T(8,128)(2,1)} fusion(pred[256,64]{0,1:T(8,128)(4,1)S(1)} %iota_compare_fusion.1, bf16[256,64]{0,1:T(8,128)(2,1)S(1)} %psum.7), kind=kLoop, calls=%fused_computation.10 | loop fusion | flops 1048576 | bytes 2146304 | tf_op jit(solution)/shard_map/jit(_where)/select_n | solution.py:55
  83.4 2.6 %select_n.53 = bf16[2,128,4096]{1,0,2:T(2,128)(2,1)S(1)} reshape(bf16[256,64,64]{0,2,1:T(8,128)(2,1)} %broadcast_select_fusion) | data formatting | bytes 4194304 | tf_op jit(solution)/shard_map/jit(_where)/select_n | solution.py:55
  86.0 5.7 %fusion.4 = f32[2,128,1024]{2,1,0:T(8,128)S(1)} fusion(bf16[4096,1024,1]{1,0,2:T(8,128)(2,1)} %bitcast.73, bf16[2,128,4096]{1,0,2:T(2,128)(2,1)S(1)} %select_n.53), kind=kOutput, calls=%fused_computation.8 | convolution fusion | flops 2147483648 | bytes 11534336 | tf_op jit(solution)/shard_map/dot_general | solution.py:57
  91.7 4.6 %all_to_all.10 = f32[2,128,1024]{2,1,0:T(8,128)S(1)} all-to-all(f32[2,128,1024]{2,1,0:T(8,128)S(1)} %fusion.4), channel_id=1, replica_groups=mesh['parts'=2,'dp'=2,'tensor'=8] {'dp'}, dimensions={0} | all-to-all | bytes 2097152 | tf_op jit(solution)/shard_map/all_to_all | solution.py:110
  96.3 0.1 reduce_sum.39
  96.4 24.1 %reduce-scatter.2.cloned.1.call-done = f32[1024,128]{0,1:T(8,128)} async-done(((f32[8192,128]{0,1:T(8,128)}), f32[1024,128]{0,1:T(8,128)}) %reduce-scatter.2.cloned.1.call-update) | async-done | bytes 524304 | tf_op jit(solution)/shard_map/reduce_scatter | solution.py:73
  120.5 1.8 %fusion.11 = bf16[128,1024]{1,0:T(8,128)(2,1)} fusion(f32[128,1024]{1,0:T(8,128)S(1)} %reduce_sum.39, f32[1024,128]{0,1:T(8,128)} %reduce-scatter.2.cloned.1.call-done), kind=kLoop, calls=%fused_computation.15 | loop fusion | flops 262144 | bytes 1310720 | tf_op jit(solution)/shard_map/convert_element_type | solution.py:112
  (15 shorter events, 0.4 us)
Async XLA Ops:
  6.5 114.0 %reduce-scatter.2.cloned.1.call-start = ((), (), s32[]{:S(2)}) async-start(), calls=%async_computation.3 | async-start | bytes 4718592 | tf_op jit(solution)/shard_map/reduce_scatter | solution.py:73
  27.6 0.7 copy-start
  27.6 0.7 copy-start.1
  29.4 5.2 %all-to-all-start = ((bf16[2,128,1024]{2,1,0:T(8,128)(2,1)}), bf16[2,128,1024]{2,1,0:T(8,128)(2,1)S(1)}, u32[]{:S(2)}, u32[]{:S(2)}) async-start(bf16[2,128,1024]{2,1,0:T(8,128)(2,1)} %broadcast_select_fusion.1), calls=%async_computation.1 | async-start | bytes 1048576 | tf_op jit(solution)/shard_map/all_to_all | solution.py:98
Sparse Core Ops, SparseCore 0:
  27.7 92.7 reduce-scatter.1
where the time goes:
time: 130 us; the launch traced here: 129 us
  blocking collectives  45.7 us (35%)
  matrix products  30.2 us (23%)
  waiting for transfers between devices  25.8 us (20%)
  between operations  13.5 us (10%)
  other arithmetic  5.76 us (4%)
  local copies, waits for them, and re-layouts  4.71 us (4%)
  starting transfers between devices  3.49 us (3%)
    psum x1, blocking collectives, rank_delta(): low = lax.psum(picked, 'tensor').astype(jnp.bfloat16)  41.1 us
    reduce_scatter x1, waiting for transfers between devices, on_device(): lax.psum_scatter(lax.dot_general(output_projection_weight, attention_resu...  24.1 us
    dot_general x1, matrix products, on_device(): lax.dot_general(output_projection_weight, attention_result, (((0,), (1,))...  10.1 us
    dot_general x1, matrix products, rank_delta(): jnp.dot(features, down_flat, preferred_element_type=jnp.float32)  6.09 us
    dot_general x1, matrix products, rank_delta(): return jnp.dot(widened_rows, up_flat, preferred_element_type=jnp.float32)  5.74 us
    all_to_all x1, blocking collectives, on_device(): lax.all_to_all(terms, 'dp', split_axis=0, concat_axis=0, tiled=True)  4.58 us
    dot_general x1, matrix products, attend(): jnp.einsum('rsgd,rcsd->rsgc', heads, cache[..., :head_width], preferred_e...  4.54 us
    all_to_all x1, starting transfers between devices, on_device(): lax.all_to_all(outgoing, 'dp', split_axis=0, concat_axis=0, tiled=True)  3.49 us
  transfers between devices with their start and end apart: 2, of which 2 were waited for; matrix products, arithmetic and copies ran while one was open for 13% of the time, Pallas kernels for 0%

commit v1 on v0

v1 whole, which is shorter than its diff:
```python
import functools
import math

import jax
import jax.numpy as jnp
from jax import lax
from jax.experimental import pallas as pl
from jax.experimental.pallas import tpu as pltpu
from jax.sharding import PartitionSpec as P

MESH = pl.DeviceIdType.MESH


def attend(query, step_key_value, cache):
    row_count = query.shape[0]
    copies = cache.shape[2]
    head_width = cache.shape[3] // 2
    group = query.shape[1] // (copies * head_width)
    heads = query.reshape(row_count, copies, group, head_width)
    score_scale = 1.0 / math.sqrt(head_width)
    scores = (
        jnp.einsum(
            "rsgd,rcsd->rsgc", heads, cache[..., :head_width], preferred_element_type=jnp.float32
        )
        * score_scale
    )
    own_score = (
        jnp.einsum(
            "rsgd,rsd->rsg",
            heads,
            step_key_value[..., :head_width],
            preferred_element_type=jnp.float32,
        )
        * score_scale
    )
    peak = jnp.maximum(jnp.max(scores, axis=-1), own_score)
    expos = jnp.exp(scores - peak[..., None])
    own_expo = jnp.exp(own_score - peak)
    total = jnp.sum(expos, axis=-1) + own_expo
    weights = (expos / total[..., None]).astype(jnp.bfloat16)
    own_weight = (own_expo / total).astype(jnp.bfloat16)
    summed = jnp.einsum(
        "rsgc,rcsd->rsgd", weights, cache[..., head_width:], preferred_element_type=jnp.float32
    )
    summed = summed + own_weight.astype(jnp.float32)[..., None] * step_key_value[
        :, :, None, head_width:
    ].astype(jnp.float32)
    return summed.astype(jnp.bfloat16).reshape(row_count, -1)


def flip(index, stage):
    step = 1 << stage
    bit = lax.rem(lax.div(index, step), 2)
    return index + step - 2 * step * bit


def low_stage(relative):
    return (relative & -relative).bit_length() - 1


def project(
    n, att_ref, code_ref, w_hbm, down_hbm, up_hbm, out_ref,
    w_buf, down_buf, up_buf, rows_all, send_buf, recv_buf, low_send, low_recv,
    delta, delta_send, delta_recv,
    w_sem, down_sem, up_sem, send_sem, recv_sem, low_ssem, low_rsem, pair_ssem, pair_rsem,
):
    stages = n.bit_length() - 1
    t = lax.axis_index("tensor")
    other_core = 1 - lax.axis_index("dp")
    rows, width = att_ref.shape[0], out_ref.shape[1]
    pieces, piece = down_sem.shape[0], down_buf.shape[0] // down_sem.shape[0]
    tile = min(width, 512)
    half = 64

    def load_w(x):
        block = t
        for s in range(stages):
            if (x >> s) & 1:
                block = flip(block, s)
        return pltpu.make_async_copy(
            w_hbm.at[:, pl.ds(pl.multiple_of(block * width, width), width)],
            w_buf.at[x],
            w_sem.at[x],
        )

    def load_piece(src, dst, sem, i):
        span = pl.ds(pl.multiple_of(i * piece, piece), piece)
        return pltpu.make_async_copy(src.at[span], dst.at[span], sem.at[i])

    odd = list(range(n - 1, 0, -2))
    even = list(range(n - 2, -1, -2))
    order = [odd[0]]
    for i in range(len(even) - 1):
        order += [odd[i + 1], even[i]]
    order += [0]

    load_w(order[0]).start()
    for i in range(pieces):
        load_piece(down_hbm, down_buf, down_sem, i).start()
    for x in order[1:4]:
        load_w(x).start()

    barrier = pltpu.get_barrier_semaphore()
    for s in range(stages):
        pl.semaphore_signal(barrier, inc=1, device_id={"tensor": flip(t, s)}, device_id_type=MESH)
    pl.semaphore_signal(barrier, inc=1, device_id={"dp": other_core}, device_id_type=MESH)
    pl.semaphore_wait(barrier, stages + 1)

    swap = pltpu.make_async_remote_copy(
        src_ref=att_ref,
        dst_ref=rows_all.at[pl.ds(rows, rows)],
        send_sem=pair_ssem.at[0],
        recv_sem=pair_rsem.at[0],
        device_id={"dp": other_core},
        device_id_type=MESH,
    )
    swap.start()
    rows_all[pl.ds(0, rows), :] = att_ref[...]

    def block_copy(x):
        return pltpu.make_async_remote_copy(
            src_ref=send_buf.at[x - 1],
            dst_ref=recv_buf.at[x - 1],
            send_sem=send_sem.at[x - 1],
            recv_sem=recv_sem.at[x - 1],
            device_id={"tensor": flip(t, low_stage(x))},
            device_id_type=MESH,
        )

    def step(x):
        load_w(x).wait()
        arrived = [x + (1 << s) for s in range(low_stage(x) if x else stages)]
        for a in arrived:
            block_copy(a).wait_recv()

        @pl.loop(0, width // tile)
        def _(j):
            cols = pl.ds(pl.multiple_of(j * tile, tile), tile)
            part = jnp.dot(
                att_ref[...], w_buf[x, :, cols], preferred_element_type=jnp.float32
            )
            for a in arrived:
                part = part + recv_buf[a - 1, :, cols].astype(jnp.float32)
            if x:
                send_buf[x - 1, :, cols] = part.astype(jnp.bfloat16)
            else:
                part = part + delta[pl.ds(0, rows), cols]
                part = part + delta_recv[:, cols].astype(jnp.float32)
                out_ref[:, cols] = part.astype(jnp.bfloat16)

        if x:
            block_copy(x).start()

    def low_copy(s):
        return pltpu.make_async_remote_copy(
            src_ref=low_send.at[s],
            dst_ref=low_recv.at[s],
            send_sem=low_ssem.at[s],
            recv_sem=low_rsem.at[s],
            device_id={"tensor": flip(t, s)},
            device_id_type=MESH,
        )

    first_lanes = lax.broadcasted_iota(jnp.int32, (rows, 2 * half), 1) < half

    def down():
        swap.wait_recv()

        def body(i, acc):
            load_piece(down_hbm, down_buf, down_sem, i).wait()
            span = pl.ds(pl.multiple_of(i * piece, piece), piece)
            got = lax.dot_general(
                rows_all[...], down_buf[span, :], (((1,), (1,)), ((), ())),
                preferred_element_type=jnp.float32,
            )
            for q in range(piece // (2 * half)):
                mine = code_ref[...] == i * (piece // (2 * half)) + q
                acc = acc + jnp.where(mine, got[:, 2 * half * q : 2 * half * (q + 1)], 0.0)
            return acc

        acc = lax.fori_loop(0, pieces, body, jnp.zeros((2 * rows, 2 * half), jnp.float32))
        acc = acc + pltpu.roll(acc, half, 1)
        low_send[0] = jnp.where(first_lanes, acc[:rows], acc[rows:])
        low_copy(0).start()

    def low_step(s):
        low_copy(s).wait_recv()
        low_send[s + 1] = low_send[s] + low_recv[s]
        if s + 1 < stages:
            low_copy(s + 1).start()

    back = pltpu.make_async_remote_copy(
        src_ref=delta_send,
        dst_ref=delta_recv,
        send_sem=pair_ssem.at[1],
        recv_sem=pair_rsem.at[1],
        device_id={"dp": other_core},
        device_id_type=MESH,
    )

    def up():
        packed = low_send[stages].astype(jnp.bfloat16).astype(jnp.float32)
        turned = pltpu.roll(packed, half, 1)
        low = jnp.concatenate(
            [jnp.where(first_lanes, packed, turned), jnp.where(first_lanes, turned, packed)], axis=0
        )
        delta[...] = jnp.zeros_like(delta)

        @pl.loop(0, pieces)
        def _(i):
            load_piece(up_hbm, up_buf, up_sem, i).wait()
            span = pl.ds(pl.multiple_of(i * piece, piece), piece)
            wide = jnp.concatenate(
                [
                    jnp.where(code_ref[...] == i * (piece // (2 * half)) + q, low, 0.0).astype(
                        jnp.bfloat16
                    )
                    for q in range(piece // (2 * half))
                ],
                axis=1,
            )
            delta[...] += jnp.dot(wide, up_buf[span, :], preferred_element_type=jnp.float32)

        delta_send[...] = delta[pl.ds(rows, rows), :].astype(jnp.bfloat16)
        back.start()

    step(order[0])
    for x in order[4:]:
        load_w(x).start()
    for i in range(pieces):
        load_piece(up_hbm, up_buf, up_sem, i).start()
    down()
    done = 0
    for at, x in enumerate(order[1:]):
        if x == 0:
            while done < stages:
                low_step(done)
                done += 1
                if done == stages:
                    up()
            back.wait_recv()
        step(x)
        if at >= 1 and done < stages:
            low_step(done)
            done += 1
            if done == stages:
                up()

    for x in range(1, n):
        block_copy(x).wait_send()
    for s in range(stages):
        low_copy(s).wait_send()
    swap.wait_send()
    back.wait_send()


def on_device(
    n,
    query,
    step_key_value,
    cache,
    output_projection_weight,
    adapter_down_weight,
    adapter_up_weight,
    row_adapter_index,
    adapter_storage_slot,
):
    att = attend(query, step_key_value, cache)
    rows, depth = att.shape
    width = output_projection_weight.shape[1] // n
    adapter_total = adapter_storage_slot.shape[0]
    matches = row_adapter_index[:, None] == jnp.arange(adapter_total, dtype=jnp.int32)[None, :]
    slot_all = jnp.sum(jnp.where(matches, adapter_storage_slot[None, :], 0), axis=1)
    me = lax.axis_index("dp")
    slots_here = adapter_up_weight.shape[0]
    rank = adapter_up_weight.shape[1]
    slots = jnp.concatenate(
        [
            lax.dynamic_slice_in_dim(slot_all, me * rows, rows),
            lax.dynamic_slice_in_dim(slot_all, (1 - me) * rows, rows),
        ]
    )
    local = slots - me * slots_here
    held = (local >= 0) & (local < slots_here)
    lane_half = (jnp.arange(2 * rank, dtype=jnp.int32) // rank)[None, :]
    code = jnp.where(held[:, None] & (local[:, None] % 2 == lane_half), local[:, None] // 2, -1)
    down_rows = adapter_down_weight.transpose(1, 2, 0).reshape(-1, depth)
    up_rows = adapter_up_weight.reshape(-1, width)
    stages = n.bit_length() - 1
    wide = down_rows.shape[0]
    pieces = 8
    vmem = pl.BlockSpec(memory_space=pltpu.VMEM)
    hbm = pl.BlockSpec(memory_space=pl.ANY)
    bf16, f32 = jnp.bfloat16, jnp.float32
    dma = pltpu.SemaphoreType.DMA
    return pl.pallas_call(
        functools.partial(project, n),
        out_shape=jax.ShapeDtypeStruct((rows, width), bf16),
        in_specs=[vmem, vmem, hbm, hbm, hbm],
        out_specs=vmem,
        scratch_shapes=[
            pltpu.VMEM((n, depth, width), bf16),
            pltpu.VMEM((wide, depth), bf16),
            pltpu.VMEM((wide, width), bf16),
            pltpu.VMEM((2 * rows, depth), bf16),
            pltpu.VMEM((n - 1, rows, width), bf16),
            pltpu.VMEM((n - 1, rows, width), bf16),
            pltpu.VMEM((stages + 1, rows, 2 * rank), f32),
            pltpu.VMEM((stages, rows, 2 * rank), f32),
            pltpu.VMEM((2 * rows, width), f32),
            pltpu.VMEM((rows, width), bf16),
            pltpu.VMEM((rows, width), bf16),
            dma((n,)),
            dma((pieces,)),
            dma((pieces,)),
            dma((n - 1,)),
            dma((n - 1,)),
            dma((stages,)),
            dma((stages,)),
            dma((2,)),
            dma((2,)),
        ],
        compiler_params=pltpu.CompilerParams(
            collective_id=0, has_side_effects=True, vmem_limit_bytes=52 * 1024 * 1024
        ),
        cost_estimate=pl.CostEstimate(
            flops=2 * rows * depth * width * n + 8 * rows * wide * depth,
            bytes_accessed=2 * (depth * width * n + 2 * wide * depth),
            transcendentals=0,
        ),
    )(att, code, output_projection_weight, down_rows, up_rows)


def solution(mesh):
    in_specs = (
        P(("parts", "dp"), "tensor"),
        P(("parts", "dp"), "tensor", None),
        P(("parts", "dp"), None, "tensor", None),
        P("tensor", None),
        P("tensor", "dp", None),
        P("dp", None, "tensor"),
        P("parts"),
        P(),
    )
    out_specs = P(("parts", "dp"), "tensor")
    return jax.shard_map(
        functools.partial(on_device, mesh.shape["tensor"]),
        mesh=mesh,
        in_specs=in_specs,
        out_specs=out_specs,
        check_vma=False,
    )
```

time: 130 us -> 56 us (0.43)
  blocking collectives: 45.7 us -> 0 us
  Pallas kernels: 0 us -> 43.5 us
  waiting for transfers between devices: 25.8 us -> 0 us
  matrix products: 30.2 us -> 8.25 us
  between operations: 13.5 us -> 0.11 us
  other arithmetic: 5.76 us -> 1.59 us
  starting transfers between devices: 3.49 us -> 0 us
  local copies, waits for them, and re-layouts: 4.71 us -> 2.35 us
    pallas_call x0 -> x1, Pallas kernels: none -> 43.5 us  [on_device(): pl.pallas_call(functools.partial(project, n), out_shape=jax.ShapeDtypeStr...]
    psum x1 -> x0, blocking collectives: 41.1 us -> none  [rank_delta(): low = lax.psum(picked, 'tensor').astype(jnp.bfloat16)]
    reduce_scatter x1 -> x0, waiting for transfers between devices: 24.1 us -> none  [on_device(): lax.psum_scatter(lax.dot_general(output_projection_weight, attention_resu...]
    dot_general x3 -> x0, matrix products: 21.9 us -> none  [the longest x1 10.1 us: on_device(): lax.dot_general(output_projection_weight, attention_result, (((0,), (1,))...]
    all_to_all x1 -> x0, blocking collectives: 4.58 us -> none  [on_device(): lax.all_to_all(terms, 'dp', split_axis=0, concat_axis=0, tiled=True)]
    all_to_all x1 -> x0, starting transfers between devices: 3.49 us -> none  [on_device(): lax.all_to_all(outgoing, 'dp', split_axis=0, concat_axis=0, tiled=True)]
    select_n x1 -> x0, local copies, waits for them, and re-layouts: 2.58 us -> none  [rank_delta(): jnp.where(one_hot[:, :, None], low[:, None, :], jnp.zeros((), jnp.bfloat16))]
    select_n x4 -> x3, other arithmetic: 2.48 us -> 0.19 us  [the longest x1 0.17 us: on_device(): jnp.where(held[:, None] & (local[:, None] % 2 == lane_half), local[:, Non...]
  transfers between devices with their start and end apart: 2 -> 0, of which waited for: 2 -> 0; matrix products, arithmetic and copies ran while one was open for 13% -> 0% of each run, Pallas kernels for 0% -> 0%
where the time goes in v1:
time: 56 us; the launch traced here: 55.8 us
  Pallas kernels  43.5 us (78%)
  matrix products  8.25 us (15%)
  local copies, waits for them, and re-layouts  2.35 us (4%)
  other arithmetic  1.59 us (3%)
    pallas_call x1, Pallas kernels, on_device(): pl.pallas_call(functools.partial(project, n), out_shape=jax.ShapeDtypeStr...  43.5 us
    dot_general x1, matrix products, attend(): jnp.einsum('rsgd,rcsd->rsgc', heads, cache[..., :head_width], preferred_e...  4.52 us
    dot_general x1, matrix products, attend(): jnp.einsum('rsgc,rcsd->rsgd', weights, cache[..., head_width:], preferred...  3.44 us
    unnamed x7, local copies, waits for them, and re-layouts  1.78 us

profile of v1, /device:TPU:0, one launch (start us, length us, event | category | flops | bytes accessed | tf_op | source)
XLA Modules:
  0.0 55.8 jit_solution(5207137220491505444)
XLA Ops:
  0.0 0.0 copy-start.1
  0.0 0.0 copy-start
  0.0 1.0 %copy.27 = bf16[16,8,8,128]{3,2,1,0:T(8,128)(2,1)S(1)} copy(bf16[16,8,8,128]{3,1,2,0:T(8,128)(2,1)} %bitcast.57) | data formatting | bytes 524288
  1.0 4.5 %fusion.14 = (f32[128,8]{1,0:T(8,128)S(1)}, f32[128,8,128]{2,1,0:T(8,128)S(1)}) fusion(bf16[128,8,128]{2,1,0:T(8,128)(2,1)S(1)} %bitcast.55, bf16[128,128,1,256]{3,1,0,2:T(8,128)(2,1)} %bitcast.53), kind=kOutput, calls=%fused_computation.40 | convolution fusion | flops 33815552 | bytes 4984832 | tf_op jit(solution)/shard_map/rsgd,rcsd->rsgc/dot_general | solution.py:22
  5.5 0.8 %slice_bitcast_fusion.10 = (bf16[128,128,1]{1,0,2:T(8,128)(2,1)S(1)}, f32[128,128]{1,0:T(8,128)S(1)}) fusion(bf16[128,1,256]{2,0,1:T(8,128)(2,1)} %param.9), kind=kLoop, calls=%fused_computation.19 | loop fusion | flops 16384 | bytes 163840 | tf_op jit(solution)/shard_map/reshape.8
  6.4 0.3 fusion.8
  6.8 0.1 copy.20
  6.9 0.4 fusion.5
  7.3 0.1 copy.24
  7.5 0.1 copy.22
  7.6 3.4 %fusion.4 = bf16[128,8,128]{2,1,0:T(8,128)(2,1)S(1)} fusion(bf16[128,128,1,256]{3,1,0,2:T(8,128)(2,1)} %bitcast.54, f32[128,8,128]{2,1,0:T(8,128)S(1)} %get-tuple-element.14, f32[128,128]{1,0:T(8,128)S(1)} %get-tuple-element.6, f32[128,8]{1,0:T(8,128)S(1)} %copy.24, f32[128,8]{1,0:T(8,128)S(1)} %copy.22, f32[128,8]{1,0:T(8,128)S(1)} %copy.20), kind=kOutput, calls=%fused_computation.6 | convolution fusion | flops 34340864 | bytes 5058560 | tf_op jit(solution)/shard_map/rsgc,rcsd->rsgd/dot_general | solution.py:42
  11.0 0.1 copy.32
  11.1 0.0 copy-done.1
  11.1 0.0 copy-done
  11.1 0.2 select_reduce_fusion
  11.3 0.1 fusion.13
  11.4 0.2 and_select_fusion.code_ref
  11.6 43.5 %shard_map.82 = bf16[128,1024]{1,0:T(8,128)(2,1)S(1)} custom-call(bf16[128,1024]{1,0:T(8,128)(2,1)S(1)} %bitcast.50, s32[256,128]{1,0:T(8,128)S(1)} %and_select_fusion.code_ref, bf16[1024,8192]{1,0:T(8,128)(2,1)} %w_hbm.1, bf16[4096,1024]{1,0:T(8,128)(2,1)} %bitcast.51, bf16[4096,1024]{1,0:T(8,128)(2,1)} %bitcast.52), custom_call_target="tpu_custom_call" | custom-call | flops 6442450944 | bytes 33554432 | tf_op jit(solution)/shard_map/pallas_call | solution.py:296
  55.1 0.7 %copy.34 = bf16[128,1024]{1,0:T(8,128)(2,1)} copy(bf16[128,1024]{1,0:T(8,128)(2,1)S(1)} %shard_map.82) | data formatting | bytes 524288
  (8 shorter events, 0.2 us)
Async XLA Ops:
  0.0 11.1 %copy-start.1 = (s32[128]{0:T(128)S(1)}, s32[128]{0:T(128)}, u32[]{:S(2)}) copy-start(s32[128]{0:T(128)} %param.15) | copy-start | bytes 1540
  0.0 11.1 %copy-start = (s32[256]{0:T(256)S(1)}, s32[256]{0:T(256)}, u32[]{:S(2)}) copy-start(s32[256]{0:T(256)} %param.14) | copy-start | bytes 3076

commit v2 on v1

--- a/solution.py
+++ b/solution.py
@@ -11,41 +11,8 @@
 MESH = pl.DeviceIdType.MESH
 
 
-def attend(query, step_key_value, cache):
-    row_count = query.shape[0]
-    copies = cache.shape[2]
-    head_width = cache.shape[3] // 2
-    group = query.shape[1] // (copies * head_width)
-    heads = query.reshape(row_count, copies, group, head_width)
-    score_scale = 1.0 / math.sqrt(head_width)
-    scores = (
-        jnp.einsum(
-            "rsgd,rcsd->rsgc", heads, cache[..., :head_width], preferred_element_type=jnp.float32
-        )
-        * score_scale
-    )
-    own_score = (
-        jnp.einsum(
-            "rsgd,rsd->rsg",
-            heads,
-            step_key_value[..., :head_width],
-            preferred_element_type=jnp.float32,
-        )
-        * score_scale
-    )
-    peak = jnp.maximum(jnp.max(scores, axis=-1), own_score)
-    expos = jnp.exp(scores - peak[..., None])
-    own_expo = jnp.exp(own_score - peak)
-    total = jnp.sum(expos, axis=-1) + own_expo
-    weights = (expos / total[..., None]).astype(jnp.bfloat16)
-    own_weight = (own_expo / total).astype(jnp.bfloat16)
-    summed = jnp.einsum(
-        "rsgc,rcsd->rsgd", weights, cache[..., head_width:], preferred_element_type=jnp.float32
-    )
-    summed = summed + own_weight.astype(jnp.float32)[..., None] * step_key_value[
-        :, :, None, head_width:
-    ].astype(jnp.float32)
-    return summed.astype(jnp.bfloat16).reshape(row_count, -1)
+PARTS = 2
+UNROLL = 16
 
 
 def flip(index, stage):
@@ -59,15 +26,18 @@
 
 
 def project(
-    n, att_ref, code_ref, w_hbm, down_hbm, up_hbm, out_ref,
-    w_buf, down_buf, up_buf, rows_all, send_buf, recv_buf, low_send, low_recv,
+    n, query_ref, step_ref, code_ref, cache_hbm, w_hbm, down_hbm, up_hbm, out_ref,
+    cache_buf, heads_buf, step_buf, summed_buf, w_buf, down_buf, up_buf, rows_all, send_buf, recv_buf, low_send, low_recv,
     delta, delta_send, delta_recv,
-    w_sem, down_sem, up_sem, send_sem, recv_sem, low_ssem, low_rsem, pair_ssem, pair_rsem,
+    cache_sem, w_sem, down_sem, up_sem, send_sem, recv_sem, low_ssem, low_rsem, pair_ssem, pair_rsem,
 ):
     stages = n.bit_length() - 1
     t = lax.axis_index("tensor")
     other_core = 1 - lax.axis_index("dp")
-    rows, width = att_ref.shape[0], out_ref.shape[1]
+    rows, width = out_ref.shape
+    share = rows // PARTS
+    head_width = step_ref.shape[1] // 2
+    group = query_ref.shape[1] // head_width
     pieces, piece = down_sem.shape[0], down_buf.shape[0] // down_sem.shape[0]
     tile = min(width, 512)
     half = 64
@@ -87,18 +57,30 @@
         span = pl.ds(pl.multiple_of(i * piece, piece), piece)
         return pltpu.make_async_copy(src.at[span], dst.at[span], sem.at[i])
 
+    def load_cache(i):
+        span = pl.ds(pl.multiple_of(i * UNROLL, UNROLL), UNROLL)
+        return pltpu.make_async_copy(cache_hbm.at[span], cache_buf.at[span], cache_sem.at[i])
+
     odd = list(range(n - 1, 0, -2))
     even = list(range(n - 2, -1, -2))
     order = [odd[0]]
     for i in range(len(even) - 1):
         order += [odd[i + 1], even[i]]
     order += [0]
-
-    load_w(order[0]).start()
+    chunks = share // UNROLL
+
+    for p in range(PARTS):
+        for i in range(p * chunks, (p + 1) * chunks):
+            load_cache(i).start()
+        load_w(order[p]).start()
+    for x in order[PARTS:5]:
+        load_w(x).start()
     for i in range(pieces):
         load_piece(down_hbm, down_buf, down_sem, i).start()
-    for x in order[1:4]:
+    for x in order[5:]:
         load_w(x).start()
+    for i in range(pieces):
+        load_piece(up_hbm, up_buf, up_sem, i).start()
 
     barrier = pltpu.get_barrier_semaphore()
     for s in range(stages):
@@ -106,50 +88,90 @@
     pl.semaphore_signal(barrier, inc=1, device_id={"dp": other_core}, device_id_type=MESH)
     pl.semaphore_wait(barrier, stages + 1)
 
-    swap = pltpu.make_async_remote_copy(
-        src_ref=att_ref,
-        dst_ref=rows_all.at[pl.ds(rows, rows)],
-        send_sem=pair_ssem.at[0],
-        recv_sem=pair_rsem.at[0],
-        device_id={"dp": other_core},
-        device_id_type=MESH,
-    )
-    swap.start()
-    rows_all[pl.ds(0, rows), :] = att_ref[...]
-
-    def block_copy(x):
+    step_buf[...] = step_ref[...].astype(jnp.float32)
+    for g in range(group):
+        heads_buf[:, g, :] = query_ref[:, g * head_width : (g + 1) * head_width].astype(jnp.float32)
+    score_scale = 1.0 / math.sqrt(head_width)
+
+    def swap(p):
         return pltpu.make_async_remote_copy(
-            src_ref=send_buf.at[x - 1],
-            dst_ref=recv_buf.at[x - 1],
-            send_sem=send_sem.at[x - 1],
-            recv_sem=recv_sem.at[x - 1],
+            src_ref=rows_all.at[pl.ds(p * share, share)],
+            dst_ref=rows_all.at[pl.ds(rows + p * share, share)],
+            send_sem=pair_ssem.at[p],
+            recv_sem=pair_rsem.at[p],
+            device_id={"dp": other_core},
+            device_id_type=MESH,
+        )
+
+    def attend(p):
+        @pl.loop(p * chunks, (p + 1) * chunks)
+        def _(i):
+            load_cache(i).wait()
+            for u in range(UNROLL):
+                r = i * UNROLL + u
+                heads = heads_buf[r]
+                own = step_buf[pl.ds(r, 1), :]
+                scores = lax.dot_general(
+                    heads.astype(jnp.bfloat16), cache_buf[r, :, :head_width],
+                    (((1,), (1,)), ((), ())), preferred_element_type=jnp.float32,
+                ) * score_scale
+                own_score = jnp.sum(heads * own[:, :head_width], axis=1, keepdims=True) * score_scale
+                peak = jnp.maximum(jnp.max(scores, axis=1, keepdims=True), own_score)
+                expos = jnp.exp(scores - peak)
+                own_expo = jnp.exp(own_score - peak)
+                total = jnp.sum(expos, axis=1, keepdims=True) + own_expo
+                weights = (expos / total).astype(jnp.bfloat16)
+                own_weight = (own_expo / total).astype(jnp.bfloat16).astype(jnp.float32)
+                summed_buf[r] = (
+                    jnp.dot(
+                        weights, cache_buf[r, :, head_width:], preferred_element_type=jnp.float32
+                    )
+                    + own_weight * own[:, head_width:]
+                )
+
+        mine = pl.ds(p * share, share)
+        for g in range(group):
+            rows_all[mine, g * head_width : (g + 1) * head_width] = summed_buf[mine, g, :].astype(
+                jnp.bfloat16
+            )
+        swap(p).start()
+
+    def block_copy(x, p):
+        span = pl.ds(p * share, share)
+        return pltpu.make_async_remote_copy(
+            src_ref=send_buf.at[x - 1, span],
+            dst_ref=recv_buf.at[x - 1, span],
+            send_sem=send_sem.at[x - 1, p],
+            recv_sem=recv_sem.at[x - 1, p],
             device_id={"tensor": flip(t, low_stage(x))},
             device_id_type=MESH,
         )
 
-    def step(x):
-        load_w(x).wait()
+    def step(x, p):
+        if p == 0:
+            load_w(x).wait()
+        span = pl.ds(p * share, share)
         arrived = [x + (1 << s) for s in range(low_stage(x) if x else stages)]
         for a in arrived:
-            block_copy(a).wait_recv()
+            block_copy(a, p).wait_recv()
 
         @pl.loop(0, width // tile)
         def _(j):
             cols = pl.ds(pl.multiple_of(j * tile, tile), tile)
             part = jnp.dot(
-                att_ref[...], w_buf[x, :, cols], preferred_element_type=jnp.float32
+                rows_all[span, :], w_buf[x, :, cols], preferred_element_type=jnp.float32
             )
             for a in arrived:
-                part = part + recv_buf[a - 1, :, cols].astype(jnp.float32)
+                part = part + recv_buf[a - 1, span, cols].astype(jnp.float32)
             if x:
-                send_buf[x - 1, :, cols] = part.astype(jnp.bfloat16)
+                send_buf[x - 1, span, cols] = part.astype(jnp.bfloat16)
             else:
-                part = part + delta[pl.ds(0, rows), cols]
-                part = part + delta_recv[:, cols].astype(jnp.float32)
-                out_ref[:, cols] = part.astype(jnp.bfloat16)
+                part = part + delta[span, cols]
+                part = part + delta_recv[span, cols].astype(jnp.float32)
+                out_ref[span, cols] = part.astype(jnp.bfloat16)
 
         if x:
-            block_copy(x).start()
+            block_copy(x, p).start()
 
     def low_copy(s):
         return pltpu.make_async_remote_copy(
@@ -164,7 +186,8 @@
     first_lanes = lax.broadcasted_iota(jnp.int32, (rows, 2 * half), 1) < half
 
     def down():
-        swap.wait_recv()
+        for p in range(PARTS):
+            swap(p).wait_recv()
 
         def body(i, acc):
             load_piece(down_hbm, down_buf, down_sem, i).wait()
@@ -192,8 +215,8 @@
     back = pltpu.make_async_remote_copy(
         src_ref=delta_send,
         dst_ref=delta_recv,
-        send_sem=pair_ssem.at[1],
-        recv_sem=pair_rsem.at[1],
+        send_sem=pair_ssem.at[PARTS],
+        recv_sem=pair_rsem.at[PARTS],
         device_id={"dp": other_core},
         device_id_type=MESH,
     )
@@ -224,33 +247,37 @@
         delta_send[...] = delta[pl.ds(rows, rows), :].astype(jnp.bfloat16)
         back.start()
 
-    step(order[0])
-    for x in order[4:]:
-        load_w(x).start()
-    for i in range(pieces):
-        load_piece(up_hbm, up_buf, up_sem, i).start()
+    attend(0)
+    step(order[0], 0)
+    step(order[1], 0)
+    attend(1)
+    step(order[0], 1)
     down()
     done = 0
-    for at, x in enumerate(order[1:]):
-        if x == 0:
+    for at in range(1, n):
+        if order[at] == 0:
             while done < stages:
                 low_step(done)
                 done += 1
                 if done == stages:
                     up()
             back.wait_recv()
-        step(x)
-        if at >= 1 and done < stages:
+        if at >= 2:
+            step(order[at], 0)
+        step(order[at], 1)
+        if at >= 2 and done < stages:
             low_step(done)
             done += 1
             if done == stages:
                 up()
 
     for x in range(1, n):
-        block_copy(x).wait_send()
+        for p in range(PARTS):
+            block_copy(x, p).wait_send()
     for s in range(stages):
         low_copy(s).wait_send()
-    swap.wait_send()
+    for p in range(PARTS):
+        swap(p).wait_send()
     back.wait_send()
 
 
@@ -265,8 +292,9 @@
     row_adapter_index,
     adapter_storage_slot,
 ):
-    att = attend(query, step_key_value, cache)
-    rows, depth = att.shape
+    rows, depth = query.shape
+    context, both = cache.shape[1], cache.shape[3]
+    head_width = both // 2
     width = output_projection_weight.shape[1] // n
     adapter_total = adapter_storage_slot.shape[0]
     matches = row_adapter_index[:, None] == jnp.arange(adapter_total, dtype=jnp.int32)[None, :]
@@ -296,9 +324,13 @@
     return pl.pallas_call(
         functools.partial(project, n),
         out_shape=jax.ShapeDtypeStruct((rows, width), bf16),
-        in_specs=[vmem, vmem, hbm, hbm, hbm],
+        in_specs=[vmem, vmem, vmem, hbm, hbm, hbm, hbm],
         out_specs=vmem,
         scratch_shapes=[
+            pltpu.VMEM((rows, context, both), bf16),
+            pltpu.VMEM((rows, depth // head_width, head_width), f32),
+            pltpu.VMEM((rows, both), f32),
+            pltpu.VMEM((rows, depth // head_width, head_width), f32),
             pltpu.VMEM((n, depth, width), bf16),
             pltpu.VMEM((wide, depth), bf16),
             pltpu.VMEM((wide, width), bf16),
@@ -310,25 +342,29 @@
             pltpu.VMEM((2 * rows, width), f32),
             pltpu.VMEM((rows, width), bf16),
             pltpu.VMEM((rows, width), bf16),
+            dma((rows // UNROLL,)),
             dma((n,)),
             dma((pieces,)),
             dma((pieces,)),
-            dma((n - 1,)),
-            dma((n - 1,)),
+            dma((n - 1, PARTS)),
+            dma((n - 1, PARTS)),
             dma((stages,)),
             dma((stages,)),
-            dma((2,)),
-            dma((2,)),
+            dma((PARTS + 1,)),
+            dma((PARTS + 1,)),
         ],
         compiler_params=pltpu.CompilerParams(
-            collective_id=0, has_side_effects=True, vmem_limit_bytes=52 * 1024 * 1024
+            collective_id=0, has_side_effects=True, vmem_limit_bytes=56 * 1024 * 1024
         ),
         cost_estimate=pl.CostEstimate(
             flops=2 * rows * depth * width * n + 8 * rows * wide * depth,
             bytes_accessed=2 * (depth * width * n + 2 * wide * depth),
             transcendentals=0,
         ),
-    )(att, code, output_projection_weight, down_rows, up_rows)
+    )(
+        query, step_key_value.reshape(rows, both), code, cache.reshape(rows, context, both),
+        output_projection_weight, down_rows, up_rows,
+    )
 
 
 def solution(mesh):

time: 56 us -> 92.1 us (1.64)
  Pallas kernels: 43.5 us -> 88.5 us
  matrix products: 8.25 us -> 0 us
    pallas_call x1, Pallas kernels: 43.5 us -> 88.5 us  [on_device(): pl.pallas_call(functools.partial(project, n), out_shape=jax.ShapeDtypeStr...]
    dot_general x3 -> x0, matrix products: 8.25 us -> none  [the longest x1 4.52 us: attend(): jnp.einsum('rsgd,rcsd->rsgc', heads, cache[..., :head_width], preferred_e...]
where the time goes in v2:
time: 92.1 us; the launch traced here: 92 us
  Pallas kernels  88.5 us (96%)
  local copies, waits for them, and re-layouts  1.75 us (2%)
  other arithmetic  1.74 us (2%)
    pallas_call x1, Pallas kernels, on_device(): pl.pallas_call(functools.partial(project, n), out_shape=jax.ShapeDtypeStr...  88.5 us

profile of v2, /device:TPU:0, one launch (start us, length us, event | category | flops | bytes accessed | tf_op | source)
XLA Modules:
  0.0 92.0 jit_solution(4156777836379110899)
XLA Ops:
  0.0 0.9 select_reduce_fusion
  0.9 0.1 fusion
  1.0 0.8 and_select_fusion.code_ref
  1.8 88.5 %shard_map.82 = bf16[128,1024]{1,0:T(8,128)(2,1)} custom-call(bf16[128,1024]{1,0:T(8,128)(2,1)} %query_ref.1, bf16[128,256]{1,0:T(8,128)(2,1)} %bitcast.9, s32[256,128]{1,0:T(8,128)} %and_select_fusion.code_ref, bf16[128,128,256]{2,1,0:T(8,128)(2,1)} %bitcast.6, bf16[1024,8192]{1,0:T(8,128)(2,1)} %w_hbm.1, bf16[4096,1024]{1,0:T(8,128)(2,1)} %bitcast.7, ...), custom_call_target="tpu_custom_call" | custom-call | flops 6442450944 | bytes 33554432 | tf_op jit(solution)/shard_map/pallas_call | solution.py:324
  90.3 1.7 %copy.10 = bf16[128,1024]{1,0:T(8,128)(2,1)} copy(bf16[128,1024]{1,0:T(8,128)(2,1)} %shard_map.82) | data formatting | bytes 524288
  (3 shorter events, 0.0 us)

commit v3 on v1

--- a/solution.py
+++ b/solution.py
@@ -9,6 +9,9 @@
 from jax.sharding import PartitionSpec as P
 
 MESH = pl.DeviceIdType.MESH
+
+
+PARTS = 2
 
 
 def attend(query, step_key_value, cache):
@@ -67,7 +70,8 @@
     stages = n.bit_length() - 1
     t = lax.axis_index("tensor")
     other_core = 1 - lax.axis_index("dp")
-    rows, width = att_ref.shape[0], out_ref.shape[1]
+    rows, width = out_ref.shape
+    share = rows // PARTS
     pieces, piece = down_sem.shape[0], down_buf.shape[0] // down_sem.shape[0]
     tile = min(width, 512)
     half = 64
@@ -87,18 +91,28 @@
         span = pl.ds(pl.multiple_of(i * piece, piece), piece)
         return pltpu.make_async_copy(src.at[span], dst.at[span], sem.at[i])
 
+    def real_stage(s, p):
+        return 1 - s if p == PARTS - 1 and s < 2 else s
+
+    def real(x, p):
+        return sum(((x >> s) & 1) << real_stage(s, p) for s in range(stages))
+
+    loaded = set()
     odd = list(range(n - 1, 0, -2))
     even = list(range(n - 2, -1, -2))
-    order = [odd[0]]
-    for i in range(len(even) - 1):
-        order += [odd[i + 1], even[i]]
-    order += [0]
-
-    load_w(order[0]).start()
+    first = []
+    for x in odd + even:
+        for p in range(PARTS):
+            if real(x, p) not in first:
+                first.append(real(x, p))
+    for x in first[:3]:
+        load_w(x).start()
     for i in range(pieces):
         load_piece(down_hbm, down_buf, down_sem, i).start()
-    for x in order[1:4]:
+    for x in first[3:]:
         load_w(x).start()
+    for i in range(pieces):
+        load_piece(up_hbm, up_buf, up_sem, i).start()
 
     barrier = pltpu.get_barrier_semaphore()
     for s in range(stages):
@@ -106,50 +120,54 @@
     pl.semaphore_signal(barrier, inc=1, device_id={"dp": other_core}, device_id_type=MESH)
     pl.semaphore_wait(barrier, stages + 1)
 
-    swap = pltpu.make_async_remote_copy(
-        src_ref=att_ref,
-        dst_ref=rows_all.at[pl.ds(rows, rows)],
-        send_sem=pair_ssem.at[0],
-        recv_sem=pair_rsem.at[0],
-        device_id={"dp": other_core},
-        device_id_type=MESH,
-    )
-    swap.start()
-    rows_all[pl.ds(0, rows), :] = att_ref[...]
-
-    def block_copy(x):
+    def swap(p):
         return pltpu.make_async_remote_copy(
-            src_ref=send_buf.at[x - 1],
-            dst_ref=recv_buf.at[x - 1],
-            send_sem=send_sem.at[x - 1],
-            recv_sem=recv_sem.at[x - 1],
-            device_id={"tensor": flip(t, low_stage(x))},
+            src_ref=att_ref.at[pl.ds(p * share, share)],
+            dst_ref=rows_all.at[pl.ds(rows + p * share, share)],
+            send_sem=pair_ssem.at[p],
+            recv_sem=pair_rsem.at[p],
+            device_id={"dp": other_core},
             device_id_type=MESH,
         )
 
-    def step(x):
-        load_w(x).wait()
+    def block_copy(x, p):
+        span = pl.ds(p * share, share)
+        return pltpu.make_async_remote_copy(
+            src_ref=send_buf.at[x - 1, span],
+            dst_ref=recv_buf.at[x - 1, span],
+            send_sem=send_sem.at[x - 1, p],
+            recv_sem=recv_sem.at[x - 1, p],
+            device_id={"tensor": flip(t, real_stage(low_stage(x), p))},
+            device_id_type=MESH,
+        )
+
+    def step(x, p):
+        held = real(x, p)
+        if held not in loaded:
+            loaded.add(held)
+            load_w(held).wait()
+        span = pl.ds(p * share, share)
         arrived = [x + (1 << s) for s in range(low_stage(x) if x else stages)]
         for a in arrived:
-            block_copy(a).wait_recv()
+            block_copy(a, p).wait_recv()
 
         @pl.loop(0, width // tile)
         def _(j):
             cols = pl.ds(pl.multiple_of(j * tile, tile), tile)
             part = jnp.dot(
-                att_ref[...], w_buf[x, :, cols], preferred_element_type=jnp.float32
+                rows_all[span, :], w_buf[held, :, cols], preferred_element_type=jnp.float32
             )
             for a in arrived:
-                part = part + recv_buf[a - 1, :, cols].astype(jnp.float32)
+                part = part + recv_buf[a - 1, span, cols].astype(jnp.float32)
             if x:
-                send_buf[x - 1, :, cols] = part.astype(jnp.bfloat16)
+                send_buf[x - 1, span, cols] = part.astype(jnp.bfloat16)
             else:
-                part = part + delta[pl.ds(0, rows), cols]
-                part = part + delta_recv[:, cols].astype(jnp.float32)
-                out_ref[:, cols] = part.astype(jnp.bfloat16)
+                part = part + delta[span, cols]
+                part = part + delta_recv[span, cols].astype(jnp.float32)
+                out_ref[span, cols] = part.astype(jnp.bfloat16)
 
         if x:
-            block_copy(x).start()
+            block_copy(x, p).start()
 
     def low_copy(s):
         return pltpu.make_async_remote_copy(
@@ -164,7 +182,8 @@
     first_lanes = lax.broadcasted_iota(jnp.int32, (rows, 2 * half), 1) < half
 
     def down():
-        swap.wait_recv()
+        for p in range(PARTS):
+            swap(p).wait_recv()
 
         def body(i, acc):
             load_piece(down_hbm, down_buf, down_sem, i).wait()
@@ -192,8 +211,8 @@
     back = pltpu.make_async_remote_copy(
         src_ref=delta_send,
         dst_ref=delta_recv,
-        send_sem=pair_ssem.at[1],
-        recv_sem=pair_rsem.at[1],
+        send_sem=pair_ssem.at[PARTS],
+        recv_sem=pair_rsem.at[PARTS],
         device_id={"dp": other_core},
         device_id_type=MESH,
     )
@@ -224,33 +243,41 @@
         delta_send[...] = delta[pl.ds(rows, rows), :].astype(jnp.bfloat16)
         back.start()
 
-    step(order[0])
-    for x in order[4:]:
-        load_w(x).start()
-    for i in range(pieces):
-        load_piece(up_hbm, up_buf, up_sem, i).start()
+    for p in range(PARTS):
+        swap(p).start()
+    rows_all[pl.ds(0, rows), :] = att_ref[...]
+    for x in odd[:2]:
+        for p in range(PARTS):
+            step(x, p)
     down()
+    for p in range(PARTS):
+        step(odd[2], p)
+        step(even[0], p)
+    for x in odd[3:]:
+        for p in range(PARTS):
+            step(x, p)
     done = 0
-    for at, x in enumerate(order[1:]):
-        if x == 0:
-            while done < stages:
-                low_step(done)
-                done += 1
-                if done == stages:
-                    up()
-            back.wait_recv()
-        step(x)
-        if at >= 1 and done < stages:
+    for x in even[1:-1]:
+        if done < stages - 1:
             low_step(done)
             done += 1
-            if done == stages:
-                up()
+        for p in range(PARTS):
+            step(x, p)
+    while done < stages:
+        low_step(done)
+        done += 1
+    up()
+    back.wait_recv()
+    for p in range(PARTS):
+        step(0, p)
 
     for x in range(1, n):
-        block_copy(x).wait_send()
+        for p in range(PARTS):
+            block_copy(x, p).wait_send()
     for s in range(stages):
         low_copy(s).wait_send()
-    swap.wait_send()
+    for p in range(PARTS):
+        swap(p).wait_send()
     back.wait_send()
 
 
@@ -313,12 +340,12 @@
             dma((n,)),
             dma((pieces,)),
             dma((pieces,)),
-            dma((n - 1,)),
-            dma((n - 1,)),
+            dma((n - 1, PARTS)),
+            dma((n - 1, PARTS)),
             dma((stages,)),
             dma((stages,)),
-            dma((2,)),
-            dma((2,)),
+            dma((PARTS + 1,)),
+            dma((PARTS + 1,)),
         ],
         compiler_params=pltpu.CompilerParams(
             collective_id=0, has_side_effects=True, vmem_limit_bytes=52 * 1024 * 1024
@@ -328,7 +355,9 @@
             bytes_accessed=2 * (depth * width * n + 2 * wide * depth),
             transcendentals=0,
         ),
-    )(att, code, output_projection_weight, down_rows, up_rows)
+    )(
+        att, code, output_projection_weight, down_rows, up_rows,
+    )
 
 
 def solution(mesh):

time: 56 us -> 55.5 us (level); the launches traced: 55.8 us -> 54.5 us
  Pallas kernels: 43.5 us -> 42.2 us
    pallas_call x1, Pallas kernels: 43.5 us -> 42.2 us  [on_device(): pl.pallas_call(functools.partial(project, n), out_shape=jax.ShapeDtypeStr...]
where the time goes in v3:
time: 55.5 us; the launch traced here: 54.5 us
  Pallas kernels  42.2 us (76%)
  matrix products  8.25 us (15%)
  local copies, waits for them, and re-layouts  2.35 us (4%)
  other arithmetic  1.59 us (3%)
    pallas_call x1, Pallas kernels, on_device(): pl.pallas_call(functools.partial(project, n), out_shape=jax.ShapeDtypeStr...  42.2 us
    dot_general x1, matrix products, attend(): jnp.einsum('rsgd,rcsd->rsgc', heads, cache[..., :head_width], preferred_e...  4.52 us
    dot_general x1, matrix products, attend(): jnp.einsum('rsgc,rcsd->rsgd', weights, cache[..., head_width:], preferred...  3.44 us
    unnamed x7, local copies, waits for them, and re-layouts  1.78 us

profile of v3, /device:TPU:0, one launch (start us, length us, event | category | flops | bytes accessed | tf_op | source)
XLA Modules:
  0.0 54.5 jit_solution(17940122315885575634)
XLA Ops:
  0.0 0.0 copy-start.1
  0.0 0.0 copy-start
  0.0 1.0 %copy.27 = bf16[16,8,8,128]{3,2,1,0:T(8,128)(2,1)S(1)} copy(bf16[16,8,8,128]{3,1,2,0:T(8,128)(2,1)} %bitcast.57) | data formatting | bytes 524288
  1.0 4.5 %fusion.14 = (f32[128,8]{1,0:T(8,128)S(1)}, f32[128,8,128]{2,1,0:T(8,128)S(1)}) fusion(bf16[128,8,128]{2,1,0:T(8,128)(2,1)S(1)} %bitcast.55, bf16[128,128,1,256]{3,1,0,2:T(8,128)(2,1)} %bitcast.53), kind=kOutput, calls=%fused_computation.40 | convolution fusion | flops 33815552 | bytes 4984832 | tf_op jit(solution)/shard_map/rsgd,rcsd->rsgc/dot_general | solution.py:25
  5.5 0.8 %slice_bitcast_fusion.10 = (bf16[128,128,1]{1,0,2:T(8,128)(2,1)S(1)}, f32[128,128]{1,0:T(8,128)S(1)}) fusion(bf16[128,1,256]{2,0,1:T(8,128)(2,1)} %param.9), kind=kLoop, calls=%fused_computation.19 | loop fusion | flops 16384 | bytes 163840 | tf_op jit(solution)/shard_map/reshape.8
  6.4 0.3 fusion.8
  6.8 0.1 copy.20
  6.9 0.4 fusion.5
  7.3 0.1 copy.24
  7.5 0.1 copy.22
  7.6 3.4 %fusion.4 = bf16[128,8,128]{2,1,0:T(8,128)(2,1)S(1)} fusion(bf16[128,128,1,256]{3,1,0,2:T(8,128)(2,1)} %bitcast.54, f32[128,8,128]{2,1,0:T(8,128)S(1)} %get-tuple-element.14, f32[128,128]{1,0:T(8,128)S(1)} %get-tuple-element.6, f32[128,8]{1,0:T(8,128)S(1)} %copy.24, f32[128,8]{1,0:T(8,128)S(1)} %copy.22, f32[128,8]{1,0:T(8,128)S(1)} %copy.20), kind=kOutput, calls=%fused_computation.6 | convolution fusion | flops 34340864 | bytes 5058560 | tf_op jit(solution)/shard_map/rsgc,rcsd->rsgd/dot_general | solution.py:45
  11.0 0.1 copy.32
  11.1 0.0 copy-done.1
  11.1 0.0 copy-done
  11.1 0.2 select_reduce_fusion
  11.3 0.1 fusion.13
  11.4 0.2 and_select_fusion.code_ref
  11.6 42.2 %shard_map.82 = bf16[128,1024]{1,0:T(8,128)(2,1)S(1)} custom-call(bf16[128,1024]{1,0:T(8,128)(2,1)S(1)} %bitcast.50, s32[256,128]{1,0:T(8,128)S(1)} %and_select_fusion.code_ref, bf16[1024,8192]{1,0:T(8,128)(2,1)} %w_hbm.1, bf16[4096,1024]{1,0:T(8,128)(2,1)} %bitcast.51, bf16[4096,1024]{1,0:T(8,128)(2,1)} %bitcast.52), custom_call_target="tpu_custom_call" | custom-call | flops 6442450944 | bytes 33554432 | tf_op jit(solution)/shard_map/pallas_call | solution.py:323
  53.8 0.7 %copy.34 = bf16[128,1024]{1,0:T(8,128)(2,1)} copy(bf16[128,1024]{1,0:T(8,128)(2,1)S(1)} %shard_map.82) | data formatting | bytes 524288
  (8 shorter events, 0.2 us)
Async XLA Ops:
  0.0 11.1 %copy-start.1 = (s32[128]{0:T(128)S(1)}, s32[128]{0:T(128)}, u32[]{:S(2)}) copy-start(s32[128]{0:T(128)} %param.15) | copy-start | bytes 1540
  0.0 11.1 %copy-start = (s32[256]{0:T(256)S(1)}, s32[256]{0:T(256)}, u32[]{:S(2)}) copy-start(s32[256]{0:T(256)} %param.14) | copy-start | bytes 3076

commit v4 on v3

--- a/solution.py
+++ b/solution.py
@@ -105,11 +105,11 @@
         for p in range(PARTS):
             if real(x, p) not in first:
                 first.append(real(x, p))
-    for x in first[:3]:
+    for x in first[: n // 2 + 1]:
         load_w(x).start()
     for i in range(pieces):
         load_piece(down_hbm, down_buf, down_sem, i).start()
-    for x in first[3:]:
+    for x in first[n // 2 + 1 :]:
         load_w(x).start()
     for i in range(pieces):
         load_piece(up_hbm, up_buf, up_sem, i).start()
@@ -246,16 +246,12 @@
     for p in range(PARTS):
         swap(p).start()
     rows_all[pl.ds(0, rows), :] = att_ref[...]
-    for x in odd[:2]:
+    for x in odd:
         for p in range(PARTS):
             step(x, p)
     down()
     for p in range(PARTS):
-        step(odd[2], p)
         step(even[0], p)
-    for x in odd[3:]:
-        for p in range(PARTS):
-            step(x, p)
     done = 0
     for x in even[1:-1]:
         if done < stages - 1:

time: 55.5 us -> 57.4 us (1.034)
  Pallas kernels: 42.2 us -> 44.2 us
    pallas_call x1, Pallas kernels: 42.2 us -> 44.2 us  [on_device(): pl.pallas_call(functools.partial(project, n), out_shape=jax.ShapeDtypeStr...]
where the time goes in v4:
time: 57.4 us; the launch traced here: 56.5 us
  Pallas kernels  44.2 us (77%)
  matrix products  8.25 us (14%)
  local copies, waits for them, and re-layouts  2.35 us (4%)
  other arithmetic  1.59 us (3%)
    pallas_call x1, Pallas kernels, on_device(): pl.pallas_call(functools.partial(project, n), out_shape=jax.ShapeDtypeStr...  44.2 us
    dot_general x1, matrix products, attend(): jnp.einsum('rsgd,rcsd->rsgc', heads, cache[..., :head_width], preferred_e...  4.52 us
    dot_general x1, matrix products, attend(): jnp.einsum('rsgc,rcsd->rsgd', weights, cache[..., head_width:], preferred...  3.44 us
    unnamed x7, local copies, waits for them, and re-layouts  1.78 us

profile of v4, /device:TPU:0, one launch (start us, length us, event | category | flops | bytes accessed | tf_op | source)
XLA Modules:
  0.0 56.5 jit_solution(16418150277025525856)
XLA Ops:
  0.0 0.0 copy-start.1
  0.0 0.0 copy-start
  0.0 1.0 %copy.27 = bf16[16,8,8,128]{3,2,1,0:T(8,128)(2,1)S(1)} copy(bf16[16,8,8,128]{3,1,2,0:T(8,128)(2,1)} %bitcast.57) | data formatting | bytes 524288
  1.0 4.5 %fusion.14 = (f32[128,8]{1,0:T(8,128)S(1)}, f32[128,8,128]{2,1,0:T(8,128)S(1)}) fusion(bf16[128,8,128]{2,1,0:T(8,128)(2,1)S(1)} %bitcast.55, bf16[128,128,1,256]{3,1,0,2:T(8,128)(2,1)} %bitcast.53), kind=kOutput, calls=%fused_computation.40 | convolution fusion | flops 33815552 | bytes 4984832 | tf_op jit(solution)/shard_map/rsgd,rcsd->rsgc/dot_general | solution.py:25
  5.5 0.8 %slice_bitcast_fusion.10 = (bf16[128,128,1]{1,0,2:T(8,128)(2,1)S(1)}, f32[128,128]{1,0:T(8,128)S(1)}) fusion(bf16[128,1,256]{2,0,1:T(8,128)(2,1)} %param.9), kind=kLoop, calls=%fused_computation.19 | loop fusion | flops 16384 | bytes 163840 | tf_op jit(solution)/shard_map/reshape.8
  6.4 0.3 fusion.8
  6.8 0.1 copy.20
  6.9 0.4 fusion.5
  7.3 0.1 copy.24
  7.5 0.1 copy.22
  7.6 3.4 %fusion.4 = bf16[128,8,128]{2,1,0:T(8,128)(2,1)S(1)} fusion(bf16[128,128,1,256]{3,1,0,2:T(8,128)(2,1)} %bitcast.54, f32[128,8,128]{2,1,0:T(8,128)S(1)} %get-tuple-element.14, f32[128,128]{1,0:T(8,128)S(1)} %get-tuple-element.6, f32[128,8]{1,0:T(8,128)S(1)} %copy.24, f32[128,8]{1,0:T(8,128)S(1)} %copy.22, f32[128,8]{1,0:T(8,128)S(1)} %copy.20), kind=kOutput, calls=%fused_computation.6 | convolution fusion | flops 34340864 | bytes 5058560 | tf_op jit(solution)/shard_map/rsgc,rcsd->rsgd/dot_general | solution.py:45
  11.0 0.1 copy.32
  11.1 0.0 copy-done.1
  11.1 0.0 copy-done
  11.1 0.2 select_reduce_fusion
  11.3 0.1 fusion.13
  11.4 0.2 and_select_fusion.code_ref
  11.6 44.2 %shard_map.82 = bf16[128,1024]{1,0:T(8,128)(2,1)S(1)} custom-call(bf16[128,1024]{1,0:T(8,128)(2,1)S(1)} %bitcast.50, s32[256,128]{1,0:T(8,128)S(1)} %and_select_fusion.code_ref, bf16[1024,8192]{1,0:T(8,128)(2,1)} %w_hbm.1, bf16[4096,1024]{1,0:T(8,128)(2,1)} %bitcast.51, bf16[4096,1024]{1,0:T(8,128)(2,1)} %bitcast.52), custom_call_target="tpu_custom_call" | custom-call | flops 6442450944 | bytes 33554432 | tf_op jit(solution)/shard_map/pallas_call | solution.py:319
  55.8 0.7 %copy.34 = bf16[128,1024]{1,0:T(8,128)(2,1)} copy(bf16[128,1024]{1,0:T(8,128)(2,1)S(1)} %shard_map.82) | data formatting | bytes 524288
  (8 shorter events, 0.2 us)
Async XLA Ops:
  0.0 11.1 %copy-start.1 = (s32[128]{0:T(128)S(1)}, s32[128]{0:T(128)}, u32[]{:S(2)}) copy-start(s32[128]{0:T(128)} %param.15) | copy-start | bytes 1540
  0.0 11.1 %copy-start = (s32[256]{0:T(256)S(1)}, s32[256]{0:T(256)}, u32[]{:S(2)}) copy-start(s32[256]{0:T(256)} %param.14) | copy-start | bytes 3076
